TPU v7x, 512 devices: a whole 4x8x8 slice. The times are simulated.
512 devices in a mesh: tm: 64 (over z_hi, x, y), space: 8 (over z_lo, core).
Axes of the slice: x: 4, y: 8, z: 8 (z_hi: 2, z_lo: 4; z = z_hi * 4 + z_lo), core: 2. Of those that a mesh axis runs over, the one named last changes fastest.
Arguments:
- starts: float32 [64, 16, 96, 128], P('tm', 'space'), may hold values from -1 to 1
Outputs:
- ends: float32 [64, 16, 96, 128], P('tm', 'space')
All inputs are finite; a program needn't handle non-finite values.
Results may differ from a plain program's by a relative error of at most 0.00002.
Values sent between devices are 32-bit elements; how exact they have to be, the bound alone decides.
A program may use at most 64 MiB of HBM per device.

v0:
```python
import jax
import jax.numpy as jnp
from jax import lax
from jax.sharding import PartitionSpec as P

FSTEPS = 10


def extended(cells, sides, width):
    for axis, dim in sides:
        count = lax.axis_size(axis)
        head = lax.slice_in_dim(cells, 0, width, axis=dim)
        tail = lax.slice_in_dim(cells, cells.shape[dim] - width, cells.shape[dim], axis=dim)
        cells = jnp.concatenate(
            [
                lax.ppermute(tail, axis, [(i, (i + 1) % count) for i in range(count)]),
                cells,
                lax.ppermute(head, axis, [((i + 1) % count, i) for i in range(count)]),
            ],
            axis=dim,
        )
    return cells


def passed_along(block, axis, distance):
    devices = range(lax.axis_size(axis))
    route = [(i - distance, i) for i in devices if i - distance in devices]
    return lax.ppermute(block, axis, route)


def inner_step(padded, rate, react):
    center = padded[1:-1]
    plus_z = padded[2:]
    minus_z = padded[:-2]
    plus_y = jnp.roll(center, -1, 1)
    minus_y = jnp.roll(center, 1, 1)
    plus_x = jnp.roll(center, -1, 2)
    minus_x = jnp.roll(center, 1, 2)
    beside = plus_z + minus_z + (plus_y + minus_y) + (plus_x + minus_x)
    return center + rate * (beside - 6.0 * center) + react * (center - center * center * center)


def fine_map(field):
    for count in range(FSTEPS):
        padded = extended(field, (("space", 0),), 1)
        field = inner_step(padded, 0.03, 0.02)
    return field


def coarse_map(field):
    padded = extended(field, (("space", 0),), 1)
    field = inner_step(padded, 0.15, 0.1)
    return field


def pass_on(state):
    return passed_along(state, "tm", 1)


def per_device(starts):
    own_start = starts[0]
    coarse_start = coarse_map(own_start)
    delta = fine_map(own_start) - coarse_start
    leading = lax.axis_index("tm") == 0

    def relay_hop(count, carried):
        result = coarse_map(carried) + delta
        arrived = pass_on(result)
        return jnp.where(leading, own_start, arrived)

    carried = lax.fori_loop(0, lax.axis_size("tm") - 1, relay_hop, own_start)
    result = coarse_map(carried) + delta
    return result[None]


def solution(mesh):
    placed = (P("tm", "space", None, None),)
    return jax.shard_map(
        per_device,
        mesh=mesh,
        in_specs=placed,
        out_specs=P("tm", "space", None, None),
        check_vma=False,
    )
```

profile of v0, /device:TPU:256, one launch (start us, length us, event | category | flops | bytes accessed | tf_op | source)
XLA Modules:
  0.0 1622.7 jit_solution(7191033958436485558)
XLA Ops:
  102.5 1507.6 %while.10 = (s32[]{:T(128)}, f32[2,96,128]{2,1,0:T(8,128)S(1)}, pred[]{:T(512)}, f32[2,96,128]{2,1,0:T(8,128)S(1)}, f32[2,96,128]{2,1,0:T(8,128)S(1)}, /*index=5*/s32[]{:T(128)}) while((s32[]{:T(128)}, f32[2,96,128]{2,1,0:T(8,128)S(1)}, pred[]{:T(512)}, f32[2,96,128]{2,1,0:T(8,128)S(1)}, f32[2,96,128]{2,1,0:T(8,128)S(1)}, ...), condition=%wide.region_1.2_spmd, body=%wide.region_0.1_spmd.sunk | while | flops 540674 | bytes 2851006 | solution.py:71
  137.6 12.8 collective-permute-done.2
  161.7 12.7 collective-permute-done.2
  185.6 12.7 collective-permute-done.2
  209.5 12.8 collective-permute-done.2
  233.5 12.7 collective-permute-done.2
  257.4 12.7 collective-permute-done.2
  281.3 12.7 collective-permute-done.2
  305.3 12.7 collective-permute-done.2
  329.2 12.7 collective-permute-done.2
  353.2 12.7 collective-permute-done.2
  377.1 12.7 collective-permute-done.2
  401.0 12.7 collective-permute-done.2
  424.9 12.7 collective-permute-done.2
  448.9 12.7 collective-permute-done.2
  472.8 12.7 collective-permute-done.2
  496.7 12.7 collective-permute-done.2
  520.7 12.7 collective-permute-done.2
  544.6 12.7 collective-permute-done.2
  568.5 12.7 collective-permute-done.2
  592.4 12.7 collective-permute-done.2
  616.4 12.7 collective-permute-done.2
  640.3 12.7 collective-permute-done.2
  664.2 12.7 collective-permute-done.2
  688.1 12.7 collective-permute-done.2
  712.1 12.7 collective-permute-done.2
  736.0 12.7 collective-permute-done.2
  759.9 12.7 collective-permute-done.2
  783.9 12.7 collective-permute-done.2
  807.8 12.7 collective-permute-done.2
  831.7 12.7 collective-permute-done.2
  855.6 12.7 collective-permute-done.2
  879.6 12.7 collective-permute-done.2
  903.5 12.7 collective-permute-done.2
  927.4 12.7 collective-permute-done.2
  951.4 12.7 collective-permute-done.2
  975.3 12.7 collective-permute-done.2
  999.2 12.7 collective-permute-done.2
  1023.1 12.7 collective-permute-done.2
  1047.1 12.7 collective-permute-done.2
  1071.0 12.7 collective-permute-done.2
  1094.9 12.7 collective-permute-done.2
  1118.9 12.7 collective-permute-done.2
  1142.8 12.7 collective-permute-done.2
  1166.7 12.7 collective-permute-done.2
  1190.6 12.7 collective-permute-done.2
  1214.6 12.7 collective-permute-done.2
  1453.8 12.7 collective-permute-done.2
  (885 shorter events, 1018.9 us)
Async XLA Ops:
  111.8 14.6 collective-permute-start.2
  135.7 14.7 collective-permute-start.2
  159.7 14.6 collective-permute-start.2
  183.7 14.6 collective-permute-start.2
  207.6 14.7 collective-permute-start.2
  231.6 14.6 collective-permute-start.2
  255.5 14.6 collective-permute-start.2
  279.4 14.7 collective-permute-start.2
  303.4 14.6 collective-permute-start.2
  327.3 14.6 collective-permute-start.2
  351.2 14.6 collective-permute-start.2
  375.2 14.6 collective-permute-start.2
  399.1 14.6 collective-permute-start.2
  423.0 14.6 collective-permute-start.2
  446.9 14.6 collective-permute-start.2
  470.9 14.6 collective-permute-start.2
  494.8 14.6 collective-permute-start.2
  518.7 14.6 collective-permute-start.2
  542.7 14.6 collective-permute-start.2
  566.6 14.6 collective-permute-start.2
  590.5 14.6 collective-permute-start.2
  614.4 14.6 collective-permute-start.2
  638.4 14.6 collective-permute-start.2
  662.3 14.6 collective-permute-start.2
  686.2 14.6 collective-permute-start.2
  710.1 14.6 collective-permute-start.2
  734.1 14.6 collective-permute-start.2
  758.0 14.6 collective-permute-start.2
  781.9 14.6 collective-permute-start.2
  805.9 14.6 collective-permute-start.2
  829.8 14.6 collective-permute-start.2
  853.7 14.6 collective-permute-start.2
  877.6 14.6 collective-permute-start.2
  901.6 14.6 collective-permute-start.2
  925.5 14.6 collective-permute-start.2
  949.4 14.6 collective-permute-start.2
  973.4 14.6 collective-permute-start.2
  997.3 14.6 collective-permute-start.2
  1021.2 14.6 collective-permute-start.2
  1045.1 14.6 collective-permute-start.2
  1069.1 14.6 collective-permute-start.2
  1093.0 14.6 collective-permute-start.2
  1116.9 14.6 collective-permute-start.2
  1140.9 14.6 collective-permute-start.2
  1164.8 14.6 collective-permute-start.2
  1188.7 14.6 collective-permute-start.2
  1356.2 14.6 collective-permute-start.2
  1451.9 14.6 collective-permute-start.2
  (164 other events, 1296.4 us)
where the time goes:
time: 1630 us; the launch traced here: 1620 us
  waiting for transfers between devices  945 us (58%)
  starting transfers between devices  644 us (40%)
    ppermute x63, waiting for transfers between devices, passed_along(): return lax.ppermute(block, axis, route)  799 us
    ppermute x74, starting transfers between devices, extended(): lax.ppermute(head, axis, [((i + 1) % count, i) for i in range(count)])  376 us
    ppermute x74, starting transfers between devices, extended(): lax.ppermute(tail, axis, [(i, (i + 1) % count) for i in range(count)])  146 us
    ppermute x63, starting transfers between devices, passed_along(): return lax.ppermute(block, axis, route)  123 us
    ppermute x74, waiting for transfers between devices, extended(): lax.ppermute(head, axis, [((i + 1) % count, i) for i in range(count)])  96.1 us
    ppermute x74, waiting for transfers between devices, extended(): lax.ppermute(tail, axis, [(i, (i + 1) % count) for i in range(count)])  49.7 us
  transfers between devices with their start and end apart: 211, of which 137 were waited for; matrix products, arithmetic and copies ran while one was open for 1% of the time, Pallas kernels for 0%

commit v1 on v0

v1 whole, which is shorter than its diff:
```python
import jax
import jax.numpy as jnp
from jax import lax
from jax.experimental import pallas as pl
from jax.experimental.pallas import tpu as pltpu
from jax.sharding import PartitionSpec as P

MESH = pl.DeviceIdType.MESH
FSTEPS = 10
GROUP = 16
TILE = 12
WIDE = TILE + 2 * FSTEPS
SPAN = TILE + 2 * GROUP
REACH = (12, 12, 8, 4)


def step(src, dst, first, last, rate, react, more=None, keep=None):
    stay = 1.0 - 6.0 * rate + react
    halves = (slice(0, 8), slice(8, 16))
    below = [src[first - 1, h] for h in halves]
    here = [src[first, h] for h in halves]
    for y in range(first, last):
        above = [src[y + 1, h] for h in halves]
        for h, turn in ((0, 1), (1, 7)):
            v, other = here[h], here[1 - h]
            beside = (
                (other + pltpu.roll(other, turn, 0))
                + (below[h] + above[h])
                + (pltpu.roll(v, 1, 1) + pltpu.roll(v, 127, 1))
            )
            out = v * (stay - react * (v * v)) + rate * beside
            if more is not None:
                out = out + more(y, halves[h])
            dst[y, halves[h]] = out
            if keep is not None:
                keep(y, h, out)
        below, here = here, above


def kernel(
    x_ref, o_ref, wrapped, gathered, u, v, base, deltas_own, deltas, s, c, out_rows,
    slab_send, slab_recv, spread_send, delta_recv, state_recv, ends_send, ends_recv,
):
    n, sp = lax.axis_index("tm"), lax.axis_index("space")
    group, k_own = n // GROUP, n % GROUP
    quarter = k_own // 4

    def chain_tm(g, tile):
        return g * GROUP + (1 - g % 2) * 8 + tile

    is_chain = n == chain_tm(group, sp)

    wrapped[:, FSTEPS : FSTEPS + 96] = x_ref[0]
    wrapped[:, 0:FSTEPS] = x_ref[0, :, 96 - FSTEPS : 96]
    wrapped[:, FSTEPS + 96 : 2 * FSTEPS + 96] = x_ref[0, :, 0:FSTEPS]
    copies = []
    for j in range(1, 8):
        to = (sp + j) % 8
        cp = pltpu.make_async_remote_copy(
            src_ref=wrapped.at[:, pl.ds(TILE * to, WIDE)],
            dst_ref=gathered.at[pl.ds(2 * sp, 2)],
            send_sem=slab_send.at[j],
            recv_sem=slab_recv.at[j],
            device_id=(n, to),
            device_id_type=MESH,
        )
        cp.start()
        copies.append(cp)
    own = pltpu.make_async_copy(
        wrapped.at[:, pl.ds(TILE * sp, WIDE)], gathered.at[pl.ds(2 * sp, 2)], slab_recv.at[0]
    )
    own.start()
    own.wait()
    for cp in copies:
        cp.wait_recv()

    flat = gathered.reshape(16 * WIDE, 128)
    for y in range(WIDE):
        u[y, 0:8] = flat[pl.ds(y, 8, stride=2 * WIDE), :]
        u[y, 8:16] = flat[pl.ds(WIDE + y, 8, stride=2 * WIDE), :]
    first, last = FSTEPS, FSTEPS + TILE
    base[...] = u[first:last]
    step(u, v, first, last, 0.15, 0.1)
    deltas_own[...] = v[first:last]
    a, b = u, v
    for i in range(FSTEPS):
        step(a, b, i + 1, WIDE - 1 - i, 0.03, 0.02)
        a, b = b, a
    deltas_own[...] = a[first:last] - deltas_own[...]

    def spread(src, dst_of, recv, g, reach, far, sends, act):
        parts = [(0, 0, TILE, GROUP)]
        parts += [(1, TILE - reach, reach, GROUP - reach), (7, 0, reach, GROUP + TILE)]
        if far:
            parts += [(2, TILE - far, far, 0), (6, 0, far, GROUP + 2 * TILE)]
        for j, (off, at, rows, to) in enumerate(parts):
            tile = (sp + off) % 8
            tm = chain_tm(g, tile)
            src_part, dst_part = src.at[pl.ds(at, rows)], dst_of.at[pl.ds(to, rows)]
            far_copy = pltpu.make_async_remote_copy(
                src_ref=src_part,
                dst_ref=dst_part,
                send_sem=spread_send.at[sends, j],
                recv_sem=recv,
                device_id=(tm, tile),
                device_id_type=MESH,
            )
            if off:
                act(far_copy)
            else:
                mine = tm == n

                @pl.when(jnp.logical_not(mine))
                def _():
                    act(far_copy)

                if act is start:

                    @pl.when(mine)
                    def _():
                        pltpu.make_async_copy(src_part, dst_part, recv).start()

    def start(cp):
        cp.start()

    def finish(cp):
        cp.wait_send()

    def spread_deltas(act):
        for q in range(4):

            @pl.when(quarter == q)
            def _():
                spread(
                    deltas_own, deltas.at[k_own], delta_recv.at[k_own],
                    group, REACH[q], 4 if q == 0 else 0, 0, act,
                )

    def spread_first(act):
        @pl.when(n == 0)
        def _():
            spread(base, s, state_recv, 0, 12, 4, 1, act)

    spread_first(start)
    spread_deltas(start)
    spread_first(finish)
    spread_deltas(finish)

    flat_out = out_rows.reshape(GROUP * 16 * 16, 128)

    @pl.when(is_chain)
    def _():
        pltpu.make_async_copy(s, s, state_recv).wait()
        for q in range(4):
            rows = TILE + 2 * REACH[q] + (8 if q == 0 else 0)

            def pair(i, _, q=q, rows=rows):
                for half, (src, dst) in enumerate(((s, c), (c, s))):
                    k = 4 * q + 2 * i + half
                    whole = deltas.at[k, pl.ds(0, rows)]
                    pltpu.make_async_copy(whole, whole, delta_recv.at[k]).wait()

                    def keep(y, h, out):
                        if GROUP <= y < GROUP + TILE:
                            flat_out[pl.ds(k * 256 + 16 * h + y - GROUP, 8, stride=32), :] = out

                    step(
                        src, dst, 4 * q + 1, SPAN - 1 - 4 * q, 0.15, 0.1,
                        lambda y, h: deltas[k, y, h], keep,
                    )
                return 0

            lax.fori_loop(0, 2, pair, 0)

        mid = s.at[pl.ds(GROUP, TILE)]

        def pass_on(act):
            @pl.when(group < 3)
            def _():
                spread(mid, s, state_recv, group + 1, 12, 4, 1, act)

        pass_on(start)

        def send(i, _):
            k, to = i // 8, i % 8
            tm = group * GROUP + k
            src = out_rows.at[pl.ds(16 * k + 2 * to, 2), pl.ds(0, TILE)]
            dst = o_ref.at[0, :, pl.ds(TILE * sp, TILE)]
            mine = jnp.logical_and(tm == n, to == sp)

            @pl.when(mine)
            def _():
                pltpu.make_async_copy(src, dst, ends_recv).start()

            @pl.when(jnp.logical_not(mine))
            def _():
                pltpu.make_async_remote_copy(
                    src_ref=src,
                    dst_ref=dst,
                    send_sem=ends_send,
                    recv_sem=ends_recv,
                    device_id=(tm, to),
                    device_id_type=MESH,
                ).start()

            return 0

        lax.fori_loop(0, 8 * GROUP, send, 0)
        pass_on(finish)
        sent = out_rows.at[pl.ds(0, 2 * (8 * GROUP - 1)), pl.ds(0, TILE)]
        pltpu.make_async_copy(sent, sent, ends_send).wait()

    for cp in copies:
        cp.wait_send()
    pltpu.make_async_copy(o_ref, o_ref, ends_recv).wait()


def per_device(starts):
    field = jnp.float32
    dma = pltpu.SemaphoreType.DMA
    return pl.pallas_call(
        kernel,
        out_shape=jax.ShapeDtypeStruct(starts.shape, starts.dtype),
        in_specs=[pl.BlockSpec(memory_space=pltpu.VMEM)],
        out_specs=pl.BlockSpec(memory_space=pl.ANY),
        scratch_shapes=[
            pltpu.VMEM((2, 96 + 2 * FSTEPS, 128), field),
            pltpu.VMEM((16, WIDE, 128), field),
            pltpu.VMEM((WIDE, 16, 128), field),
            pltpu.VMEM((WIDE, 16, 128), field),
            pltpu.VMEM((TILE, 16, 128), field),
            pltpu.VMEM((TILE, 16, 128), field),
            pltpu.VMEM((GROUP, SPAN, 16, 128), field),
            pltpu.VMEM((SPAN, 16, 128), field),
            pltpu.VMEM((SPAN, 16, 128), field),
            pltpu.VMEM((GROUP * 16, 16, 128), field),
            dma((8,)),
            dma((8,)),
            dma((2, 5)),
            dma((GROUP,)),
            dma,
            dma,
            dma,
        ],
        compiler_params=pltpu.CompilerParams(has_side_effects=True, vmem_limit_bytes=40 << 20),
    )(starts)


def solution(mesh):
    placed = P("tm", "space", None, None)
    return jax.shard_map(
        per_device, mesh=mesh, in_specs=(placed,), out_specs=placed, check_vma=False
    )
```

time: 1630 us -> 118 us (0.07)
  the two profiles are of different devices: /device:TPU:256 before, /device:TPU:279 now
where the time goes in v1:
time: 118 us
  Pallas kernels  117 us (99%)
  local copies, waits for them, and re-layouts  1.54 us (1%)
    pallas_call x1, Pallas kernels, per_device(): pl.pallas_call(kernel, out_shape=jax.ShapeDtypeStruct(starts.shape, start...  117 us

profile of v1, /device:TPU:279, one launch (start us, length us, event | category | flops | bytes accessed | tf_op | source)
XLA Modules:
  0.0 118.3 jit_solution(4060315947914018110)
XLA Ops:
  0.0 0.0 copy-start
  0.0 0.9 copy-done
  0.9 116.8 %shard_map.17 = f32[1,2,96,128]{3,2,1,0:T(8,128)S(1)} custom-call(f32[1,2,96,128]{3,2,1,0:T(8,128)S(1)} %copy-done), custom_call_target="tpu_custom_call" | custom-call | tf_op jit(solution)/shard_map/pallas_call | solution.py:221
  117.7 0.6 copy.3
Async XLA Ops:
  0.0 0.9 copy-start

commit v2 on v1

--- a/solution.py
+++ b/solution.py
@@ -7,11 +7,13 @@
 
 MESH = pl.DeviceIdType.MESH
 FSTEPS = 10
-GROUP = 16
+STARTS = (0, 8, 20, 40, 64)
+BLOCKS = len(STARTS) - 1
+SIZES = tuple(STARTS[b + 1] - STARTS[b] for b in range(BLOCKS))
+GHOST = max(SIZES)
 TILE = 12
 WIDE = TILE + 2 * FSTEPS
-SPAN = TILE + 2 * GROUP
-REACH = (12, 12, 8, 4)
+SPAN = TILE + 2 * GHOST
 
 
 def step(src, dst, first, last, rate, react, more=None, keep=None):
@@ -37,18 +39,74 @@
         below, here = here, above
 
 
+def tile_of(sp):
+    z = sp // 2
+    return jnp.where(sp % 2 == 0, z, 7 - z)
+
+
+def space_of(tile):
+    return jnp.where(tile < 4, 2 * tile, 2 * (7 - tile) + 1)
+
+
+def chain_tm(block, tile):
+    return block * 16 + (tile % 2) * 8
+
+
+def table(values, at):
+    out = values[0]
+    for i in range(1, len(values)):
+        out = jnp.where(at >= i, values[i], out)
+    return out
+
+
 def kernel(
     x_ref, o_ref, wrapped, gathered, u, v, base, deltas_own, deltas, s, c, out_rows,
     slab_send, slab_recv, spread_send, delta_recv, state_recv, ends_send, ends_recv,
 ):
     n, sp = lax.axis_index("tm"), lax.axis_index("space")
-    group, k_own = n // GROUP, n % GROUP
-    quarter = k_own // 4
-
-    def chain_tm(g, tile):
-        return g * GROUP + (1 - g % 2) * 8 + tile
-
-    is_chain = n == chain_tm(group, sp)
+    tile = tile_of(sp)
+    block = sum((n >= start).astype(jnp.int32) for start in STARTS[1:BLOCKS])
+    left = table(STARTS[1:], block) - 1 - n
+    hub = chain_tm(block, tile)
+    chain_block = n // 16
+    is_chain = n == chain_tm(chain_block, tile)
+    chain_start = table(STARTS, chain_block)
+    chain_size = table(SIZES, chain_block)
+    chain_in_own = jnp.logical_and(n >= chain_start, n < chain_start + chain_size)
+
+    barrier = pltpu.get_barrier_semaphore()
+
+    def greet(tm, space):
+        pl.semaphore_signal(barrier, inc=1, device_id=(tm, space), device_id_type=MESH)
+
+    for j in range(1, 8):
+        greet(n, (sp + j) % 8)
+    is_hub = hub == n
+
+    @pl.when(jnp.logical_not(is_hub))
+    def _():
+        greet(hub, sp)
+
+    @pl.when(is_chain)
+    def _():
+        def spoke(i, _):
+            @pl.when(chain_start + i != n)
+            def _():
+                greet(chain_start + i, sp)
+
+            return 0
+
+        lax.fori_loop(0, chain_size, spoke, 0)
+
+        @pl.when(chain_block > 0)
+        def _():
+            for off in (-2, -1, 0, 1, 2):
+                other = (tile + off) % 8
+                greet(chain_tm(chain_block - 1, other), space_of(other))
+
+    expected = 7 + jnp.where(is_hub, 0, 1)
+    spokes = chain_size - jnp.where(chain_in_own, 1, 0) + jnp.where(chain_block < BLOCKS - 1, 5, 0)
+    pl.semaphore_wait(barrier, expected + jnp.where(is_chain, spokes, 0))
 
     wrapped[:, FSTEPS : FSTEPS + 96] = x_ref[0]
     wrapped[:, 0:FSTEPS] = x_ref[0, :, 96 - FSTEPS : 96]
@@ -57,7 +115,7 @@
     for j in range(1, 8):
         to = (sp + j) % 8
         cp = pltpu.make_async_remote_copy(
-            src_ref=wrapped.at[:, pl.ds(TILE * to, WIDE)],
+            src_ref=wrapped.at[:, pl.ds(TILE * tile_of(to), WIDE)],
             dst_ref=gathered.at[pl.ds(2 * sp, 2)],
             send_sem=slab_send.at[j],
             recv_sem=slab_recv.at[j],
@@ -67,7 +125,7 @@
         cp.start()
         copies.append(cp)
     own = pltpu.make_async_copy(
-        wrapped.at[:, pl.ds(TILE * sp, WIDE)], gathered.at[pl.ds(2 * sp, 2)], slab_recv.at[0]
+        wrapped.at[:, pl.ds(TILE * tile, WIDE)], gathered.at[pl.ds(2 * sp, 2)], slab_recv.at[0]
     )
     own.start()
     own.wait()
@@ -88,21 +146,21 @@
         a, b = b, a
     deltas_own[...] = a[first:last] - deltas_own[...]
 
-    def spread(src, dst_of, recv, g, reach, far, sends, act):
-        parts = [(0, 0, TILE, GROUP)]
-        parts += [(1, TILE - reach, reach, GROUP - reach), (7, 0, reach, GROUP + TILE)]
+    def spread(src, dst_of, recv, to_block, ghost, sends, act):
+        near, far = min(ghost, TILE), max(ghost - TILE, 0)
+        parts = [(1, TILE - near, near, GHOST - near), (7, 0, near, GHOST + TILE), (0, 0, TILE, GHOST)]
         if far:
-            parts += [(2, TILE - far, far, 0), (6, 0, far, GROUP + 2 * TILE)]
-        for j, (off, at, rows, to) in enumerate(parts):
-            tile = (sp + off) % 8
-            tm = chain_tm(g, tile)
+            parts = [(2, TILE - far, far, GHOST - TILE - far), (6, 0, far, GHOST + 2 * TILE)] + parts
+        for off, at, rows, to in parts:
+            dest = (tile + off) % 8
+            tm, space = chain_tm(to_block, dest), space_of(dest)
             src_part, dst_part = src.at[pl.ds(at, rows)], dst_of.at[pl.ds(to, rows)]
             far_copy = pltpu.make_async_remote_copy(
                 src_ref=src_part,
                 dst_ref=dst_part,
-                send_sem=spread_send.at[sends, j],
+                send_sem=spread_send.at[sends, off],
                 recv_sem=recv,
-                device_id=(tm, tile),
+                device_id=(tm, space),
                 device_id_type=MESH,
             )
             if off:
@@ -127,65 +185,72 @@
         cp.wait_send()
 
     def spread_deltas(act):
-        for q in range(4):
-
-            @pl.when(quarter == q)
+        for q in range(GHOST // 4):
+
+            @pl.when(left // 4 == q)
             def _():
                 spread(
-                    deltas_own, deltas.at[k_own], delta_recv.at[k_own],
-                    group, REACH[q], 4 if q == 0 else 0, 0, act,
+                    deltas_own, deltas.at[left], delta_recv.at[left], block, 4 * q + 4, 0, act
                 )
 
     def spread_first(act):
         @pl.when(n == 0)
         def _():
-            spread(base, s, state_recv, 0, 12, 4, 1, act)
+            spread(base, s, state_recv, 0, SIZES[0], 1, act)
 
     spread_first(start)
     spread_deltas(start)
     spread_first(finish)
     spread_deltas(finish)
 
-    flat_out = out_rows.reshape(GROUP * 16 * 16, 128)
+    flat_out = out_rows.reshape(GHOST * 16 * 16, 128)
 
     @pl.when(is_chain)
     def _():
-        pltpu.make_async_copy(s, s, state_recv).wait()
-        for q in range(4):
-            rows = TILE + 2 * REACH[q] + (8 if q == 0 else 0)
-
-            def pair(i, _, q=q, rows=rows):
+        for b in range(BLOCKS):
+
+            @pl.when(chain_block == b)
+            def _():
+                whole = s.at[pl.ds(0, TILE + 2 * SIZES[b])]
+                pltpu.make_async_copy(whole, whole, state_recv).wait()
+
+        for q in reversed(range(GHOST // 4)):
+            ghost = 4 * q + 4
+
+            def pair(i, _, ghost=ghost):
                 for half, (src, dst) in enumerate(((s, c), (c, s))):
-                    k = 4 * q + 2 * i + half
-                    whole = deltas.at[k, pl.ds(0, rows)]
-                    pltpu.make_async_copy(whole, whole, delta_recv.at[k]).wait()
+                    rem = ghost - 1 - 2 * i - half
+                    whole = deltas.at[rem, pl.ds(0, TILE + 2 * ghost)]
+                    pltpu.make_async_copy(whole, whole, delta_recv.at[rem]).wait()
 
                     def keep(y, h, out):
-                        if GROUP <= y < GROUP + TILE:
-                            flat_out[pl.ds(k * 256 + 16 * h + y - GROUP, 8, stride=32), :] = out
+                        if GHOST <= y < GHOST + TILE:
+                            flat_out[pl.ds(rem * 256 + 16 * h + y - GHOST, 8, stride=32), :] = out
 
                     step(
-                        src, dst, 4 * q + 1, SPAN - 1 - 4 * q, 0.15, 0.1,
-                        lambda y, h: deltas[k, y, h], keep,
+                        src, dst, GHOST + 1 - ghost, GHOST + TILE + ghost - 1, 0.15, 0.1,
+                        lambda y, h: deltas[rem, y, h], keep,
                     )
                 return 0
 
-            lax.fori_loop(0, 2, pair, 0)
-
-        mid = s.at[pl.ds(GROUP, TILE)]
+            lax.fori_loop(0, jnp.where(chain_size >= ghost, 2, 0), pair, 0)
+
+        mid = s.at[pl.ds(GHOST, TILE)]
 
         def pass_on(act):
-            @pl.when(group < 3)
-            def _():
-                spread(mid, s, state_recv, group + 1, 12, 4, 1, act)
+            for b in range(BLOCKS - 1):
+
+                @pl.when(chain_block == b)
+                def _():
+                    spread(mid, s, state_recv, b + 1, SIZES[b + 1], 1, act)
 
         pass_on(start)
 
         def send(i, _):
-            k, to = i // 8, i % 8
-            tm = group * GROUP + k
-            src = out_rows.at[pl.ds(16 * k + 2 * to, 2), pl.ds(0, TILE)]
-            dst = o_ref.at[0, :, pl.ds(TILE * sp, TILE)]
+            rem, to = chain_size - 1 - i // 8, i % 8
+            tm = chain_start + i // 8
+            src = out_rows.at[pl.ds(16 * rem + 2 * to, 2), pl.ds(0, TILE)]
+            dst = o_ref.at[0, :, pl.ds(TILE * tile, TILE)]
             mine = jnp.logical_and(tm == n, to == sp)
 
             @pl.when(mine)
@@ -205,10 +270,15 @@
 
             return 0
 
-        lax.fori_loop(0, 8 * GROUP, send, 0)
+        lax.fori_loop(0, 8 * chain_size, send, 0)
         pass_on(finish)
-        sent = out_rows.at[pl.ds(0, 2 * (8 * GROUP - 1)), pl.ds(0, TILE)]
-        pltpu.make_async_copy(sent, sent, ends_send).wait()
+        for b in range(BLOCKS):
+            for own in (False, True):
+
+                @pl.when(jnp.logical_and(chain_block == b, chain_in_own == own))
+                def _():
+                    sent = out_rows.at[pl.ds(0, 2 * (8 * SIZES[b] - own)), pl.ds(0, TILE)]
+                    pltpu.make_async_copy(sent, sent, ends_send).wait()
 
     for cp in copies:
         cp.wait_send()
@@ -230,19 +300,21 @@
             pltpu.VMEM((WIDE, 16, 128), field),
             pltpu.VMEM((TILE, 16, 128), field),
             pltpu.VMEM((TILE, 16, 128), field),
-            pltpu.VMEM((GROUP, SPAN, 16, 128), field),
+            pltpu.VMEM((GHOST, SPAN, 16, 128), field),
             pltpu.VMEM((SPAN, 16, 128), field),
             pltpu.VMEM((SPAN, 16, 128), field),
-            pltpu.VMEM((GROUP * 16, 16, 128), field),
+            pltpu.VMEM((GHOST * 16, 16, 128), field),
             dma((8,)),
             dma((8,)),
-            dma((2, 5)),
-            dma((GROUP,)),
+            dma((2, 8)),
+            dma((GHOST,)),
             dma,
             dma,
             dma,
         ],
-        compiler_params=pltpu.CompilerParams(has_side_effects=True, vmem_limit_bytes=40 << 20),
+        compiler_params=pltpu.CompilerParams(
+            collective_id=0, has_side_effects=True, vmem_limit_bytes=40 << 20
+        ),
     )(starts)
 
 

time: 118 us -> 177 us (1.50)
  the two profiles are of different devices: /device:TPU:279 before, /device:TPU:487 now
where the time goes in v2:
time: 177 us; the launch traced here: 176 us
  Pallas kernels  175 us (99%)
    pallas_call x1, Pallas kernels, per_device(): pl.pallas_call(kernel, out_shape=jax.ShapeDtypeStruct(starts.shape, start...  175 us

profile of v2, /device:TPU:487, one launch (start us, length us, event | category | flops | bytes accessed | tf_op | source)
XLA Modules:
  0.0 176.4 jit_solution(10531915052009173444)
XLA Ops:
  0.0 0.0 copy-start
  0.0 0.9 copy-done
  0.9 174.9 %shard_map.17 = f32[1,2,96,128]{3,2,1,0:T(8,128)S(1)} custom-call(f32[1,2,96,128]{3,2,1,0:T(8,128)S(1)} %copy-done), custom_call_target="tpu_custom_call" | custom-call | tf_op jit(solution)/shard_map/pallas_call | solution.py:291
  175.8 0.6 copy.3
Async XLA Ops:
  0.0 0.9 copy-start

commit v3 on v2

--- a/solution.py
+++ b/solution.py
@@ -7,10 +7,11 @@
 
 MESH = pl.DeviceIdType.MESH
 FSTEPS = 10
-STARTS = (0, 8, 20, 40, 64)
+STARTS = (0, 8, 20, 32, 48, 64)
 BLOCKS = len(STARTS) - 1
 SIZES = tuple(STARTS[b + 1] - STARTS[b] for b in range(BLOCKS))
 GHOST = max(SIZES)
+BASES = (0, 8, 24, 32, 56)
 TILE = 12
 WIDE = TILE + 2 * FSTEPS
 SPAN = TILE + 2 * GHOST
@@ -39,17 +40,14 @@
         below, here = here, above
 
 
-def tile_of(sp):
-    z = sp // 2
+def tile_of(sp, tm):
+    z = jnp.where(tm < 32, sp // 2, 3 - sp // 2)
     return jnp.where(sp % 2 == 0, z, 7 - z)
 
 
-def space_of(tile):
-    return jnp.where(tile < 4, 2 * tile, 2 * (7 - tile) + 1)
-
-
-def chain_tm(block, tile):
-    return block * 16 + (tile % 2) * 8
+def space_of(tile, tm):
+    z = jnp.where(tile < 4, tile, 7 - tile)
+    return 2 * jnp.where(tm < 32, z, 3 - z) + jnp.where(tile < 4, 0, 1)
 
 
 def table(values, at):
@@ -64,15 +62,13 @@
     slab_send, slab_recv, spread_send, delta_recv, state_recv, ends_send, ends_recv,
 ):
     n, sp = lax.axis_index("tm"), lax.axis_index("space")
-    tile = tile_of(sp)
+    tile = tile_of(sp, n)
     block = sum((n >= start).astype(jnp.int32) for start in STARTS[1:BLOCKS])
     left = table(STARTS[1:], block) - 1 - n
-    hub = chain_tm(block, tile)
-    chain_block = n // 16
-    is_chain = n == chain_tm(chain_block, tile)
-    chain_start = table(STARTS, chain_block)
-    chain_size = table(SIZES, chain_block)
-    chain_in_own = jnp.logical_and(n >= chain_start, n < chain_start + chain_size)
+    hub = table(BASES, block) + tile
+    is_chain = hub == n
+    size = table(SIZES, block)
+    first_slice = table(STARTS, block)
 
     barrier = pltpu.get_barrier_semaphore()
 
@@ -81,32 +77,31 @@
 
     for j in range(1, 8):
         greet(n, (sp + j) % 8)
-    is_hub = hub == n
-
-    @pl.when(jnp.logical_not(is_hub))
+
+    @pl.when(jnp.logical_not(is_chain))
     def _():
         greet(hub, sp)
 
     @pl.when(is_chain)
     def _():
         def spoke(i, _):
-            @pl.when(chain_start + i != n)
-            def _():
-                greet(chain_start + i, sp)
+            @pl.when(first_slice + i != n)
+            def _():
+                greet(first_slice + i, sp)
 
             return 0
 
-        lax.fori_loop(0, chain_size, spoke, 0)
-
-        @pl.when(chain_block > 0)
+        lax.fori_loop(0, size, spoke, 0)
+
+        @pl.when(block > 0)
         def _():
+            before = table(BASES, block - 1)
             for off in (-2, -1, 0, 1, 2):
                 other = (tile + off) % 8
-                greet(chain_tm(chain_block - 1, other), space_of(other))
-
-    expected = 7 + jnp.where(is_hub, 0, 1)
-    spokes = chain_size - jnp.where(chain_in_own, 1, 0) + jnp.where(chain_block < BLOCKS - 1, 5, 0)
-    pl.semaphore_wait(barrier, expected + jnp.where(is_chain, spokes, 0))
+                greet(before + other, space_of(other, before))
+
+    spokes = size - 1 + jnp.where(block < BLOCKS - 1, 5, 0)
+    pl.semaphore_wait(barrier, 7 + jnp.where(is_chain, spokes, 1))
 
     wrapped[:, FSTEPS : FSTEPS + 96] = x_ref[0]
     wrapped[:, 0:FSTEPS] = x_ref[0, :, 96 - FSTEPS : 96]
@@ -115,7 +110,7 @@
     for j in range(1, 8):
         to = (sp + j) % 8
         cp = pltpu.make_async_remote_copy(
-            src_ref=wrapped.at[:, pl.ds(TILE * tile_of(to), WIDE)],
+            src_ref=wrapped.at[:, pl.ds(TILE * tile_of(to, n), WIDE)],
             dst_ref=gathered.at[pl.ds(2 * sp, 2)],
             send_sem=slab_send.at[j],
             recv_sem=slab_recv.at[j],
@@ -146,14 +141,14 @@
         a, b = b, a
     deltas_own[...] = a[first:last] - deltas_own[...]
 
-    def spread(src, dst_of, recv, to_block, ghost, sends, act):
+    def spread(src, dst_of, recv, base_tm, ghost, sends, act):
         near, far = min(ghost, TILE), max(ghost - TILE, 0)
         parts = [(1, TILE - near, near, GHOST - near), (7, 0, near, GHOST + TILE), (0, 0, TILE, GHOST)]
         if far:
             parts = [(2, TILE - far, far, GHOST - TILE - far), (6, 0, far, GHOST + 2 * TILE)] + parts
         for off, at, rows, to in parts:
             dest = (tile + off) % 8
-            tm, space = chain_tm(to_block, dest), space_of(dest)
+            tm, space = base_tm + dest, space_of(dest, base_tm)
             src_part, dst_part = src.at[pl.ds(at, rows)], dst_of.at[pl.ds(to, rows)]
             far_copy = pltpu.make_async_remote_copy(
                 src_ref=src_part,
@@ -190,13 +185,14 @@
             @pl.when(left // 4 == q)
             def _():
                 spread(
-                    deltas_own, deltas.at[left], delta_recv.at[left], block, 4 * q + 4, 0, act
+                    deltas_own, deltas.at[left], delta_recv.at[left],
+                    table(BASES, block), 4 * q + 4, 0, act,
                 )
 
     def spread_first(act):
         @pl.when(n == 0)
         def _():
-            spread(base, s, state_recv, 0, SIZES[0], 1, act)
+            spread(base, s, state_recv, BASES[0], SIZES[0], 1, act)
 
     spread_first(start)
     spread_deltas(start)
@@ -209,7 +205,7 @@
     def _():
         for b in range(BLOCKS):
 
-            @pl.when(chain_block == b)
+            @pl.when(block == b)
             def _():
                 whole = s.at[pl.ds(0, TILE + 2 * SIZES[b])]
                 pltpu.make_async_copy(whole, whole, state_recv).wait()
@@ -233,22 +229,22 @@
                     )
                 return 0
 
-            lax.fori_loop(0, jnp.where(chain_size >= ghost, 2, 0), pair, 0)
+            lax.fori_loop(0, jnp.where(size >= ghost, 2, 0), pair, 0)
 
         mid = s.at[pl.ds(GHOST, TILE)]
 
         def pass_on(act):
             for b in range(BLOCKS - 1):
 
-                @pl.when(chain_block == b)
+                @pl.when(block == b)
                 def _():
-                    spread(mid, s, state_recv, b + 1, SIZES[b + 1], 1, act)
+                    spread(mid, s, state_recv, BASES[b + 1], SIZES[b + 1], 1, act)
 
         pass_on(start)
 
         def send(i, _):
-            rem, to = chain_size - 1 - i // 8, i % 8
-            tm = chain_start + i // 8
+            rem, to = size - 1 - i // 8, i % 8
+            tm = first_slice + i // 8
             src = out_rows.at[pl.ds(16 * rem + 2 * to, 2), pl.ds(0, TILE)]
             dst = o_ref.at[0, :, pl.ds(TILE * tile, TILE)]
             mine = jnp.logical_and(tm == n, to == sp)
@@ -270,15 +266,14 @@
 
             return 0
 
-        lax.fori_loop(0, 8 * chain_size, send, 0)
+        lax.fori_loop(0, 8 * size, send, 0)
         pass_on(finish)
         for b in range(BLOCKS):
-            for own in (False, True):
-
-                @pl.when(jnp.logical_and(chain_block == b, chain_in_own == own))
-                def _():
-                    sent = out_rows.at[pl.ds(0, 2 * (8 * SIZES[b] - own)), pl.ds(0, TILE)]
-                    pltpu.make_async_copy(sent, sent, ends_send).wait()
+
+            @pl.when(block == b)
+            def _():
+                sent = out_rows.at[pl.ds(0, 2 * (8 * SIZES[b] - 1)), pl.ds(0, TILE)]
+                pltpu.make_async_copy(sent, sent, ends_send).wait()
 
     for cp in copies:
         cp.wait_send()

time: 177 us -> 83.2 us (0.47)
  the two profiles are of different devices: /device:TPU:487 before, /device:TPU:511 now
where the time goes in v3:
time: 83.2 us; the launch traced here: 83.1 us
  Pallas kernels  81.5 us (98%)
  local copies, waits for them, and re-layouts  1.54 us (2%)
    pallas_call x1, Pallas kernels, per_device(): pl.pallas_call(kernel, out_shape=jax.ShapeDtypeStruct(starts.shape, start...  81.5 us

profile of v3, /device:TPU:511, one launch (start us, length us, event | category | flops | bytes accessed | tf_op | source)
XLA Modules:
  0.0 83.1 jit_solution(2402604598229835714)
XLA Ops:
  0.0 0.0 copy-start
  0.0 0.9 %copy-done = f32[1,2,96,128]{3,2,1,0:T(8,128)S(1)} copy-done((f32[1,2,96,128]{3,2,1,0:T(8,128)S(1)}, f32[1,2,96,128]{3,2,1,0:T(8,128)}, u32[]{:S(2)}) %copy-start) | copy-done | bytes 98328
  0.9 81.5 %shard_map.17 = f32[1,2,96,128]{3,2,1,0:T(8,128)S(1)} custom-call(f32[1,2,96,128]{3,2,1,0:T(8,128)S(1)} %copy-done), custom_call_target="tpu_custom_call" | custom-call | tf_op jit(solution)/shard_map/pallas_call | solution.py:286
  82.4 0.6 copy.3
Async XLA Ops:
  0.0 0.9 %copy-start = (f32[1,2,96,128]{3,2,1,0:T(8,128)S(1)}, f32[1,2,96,128]{3,2,1,0:T(8,128)}, u32[]{:S(2)}) copy-start(f32[1,2,96,128]{3,2,1,0:T(8,128)} %x_ref.1) | copy-start | bytes 294916

commit v4 on v3

v4 whole, which is shorter than its diff:
```python
import functools

import jax
import jax.numpy as jnp
from jax import lax
from jax.experimental import pallas as pl
from jax.experimental.pallas import tpu as pltpu
from jax.sharding import PartitionSpec as P

MESH = pl.DeviceIdType.MESH
FSTEPS = 10
STARTS = (0, 8, 20, 32, 48, 64)
BLOCKS = len(STARTS) - 1
SIZES = tuple(STARTS[b + 1] - STARTS[b] for b in range(BLOCKS))
GHOST = max(SIZES)
PLACES = ((0, 0), (8, 8), (24, 24), (32, 40), (56, 48))
TILE = 12
WIDE = TILE + 2 * FSTEPS
SPAN = TILE + 2 * GHOST


def step(src, dst, first, last, rate, react, more=None, keep=None):
    stay = 1.0 - 6.0 * rate + react
    halves = (slice(0, 8), slice(8, 16))
    below = [src[first - 1, h] for h in halves]
    here = [src[first, h] for h in halves]
    for y in range(first, last):
        above = [src[y + 1, h] for h in halves]
        for h, turn in ((0, 1), (1, 7)):
            v, other = here[h], here[1 - h]
            beside = (
                (other + pltpu.roll(other, turn, 0))
                + (below[h] + above[h])
                + (pltpu.roll(v, 1, 1) + pltpu.roll(v, 127, 1))
            )
            out = v * (stay - react * (v * v)) + rate * beside
            if more is not None:
                out = out + more(y, halves[h])
            dst[y, halves[h]] = out
            if keep is not None:
                keep(y, h, out)
        below, here = here, above


def tile_of(sp, tm):
    z = jnp.where(tm < 32, sp // 2, 3 - sp // 2)
    return jnp.where(sp % 2 == 0, z, 7 - z)


def space_of(tile, tm):
    z = jnp.where(tile < 4, tile, 7 - tile)
    return 2 * jnp.where(tm < 32, z, 3 - z) + jnp.where(tile < 4, 0, 1)


def place(block, tile):
    low = table([at[0] for at in PLACES], block)
    return tile + jnp.where(tile < 4, low, table([at[1] for at in PLACES], block))


def table(values, at):
    out = values[0]
    for i in range(1, len(values)):
        out = jnp.where(at >= i, values[i], out)
    return out


def kernel(
    x_ref, o_ref, wrapped, gathered, u, v, fine, deltas_own, deltas, s, c, out_rows,
    slab_send, slab_recv, spread_send, delta_recv, state_recv, ends_send, ends_recv, load_sem,
):
    n, sp = lax.axis_index("tm"), lax.axis_index("space")
    tile = tile_of(sp, n)
    block = sum((n >= start).astype(jnp.int32) for start in STARTS[1:BLOCKS])
    left = table(STARTS[1:], block) - 1 - n
    hub = place(block, tile)
    carries = [n == place(b, tile) for b in range(BLOCKS)]
    is_chain = functools.reduce(jnp.logical_or, carries)
    role = sum(b * carries[b].astype(jnp.int32) for b in range(BLOCKS))
    size, first_slice = table(SIZES, role), table(STARTS, role)
    in_own = jnp.logical_and(n >= first_slice, n < first_slice + size)

    loads = [
        pltpu.make_async_copy(
            x_ref.at[0, :, pl.ds(at, rows)], wrapped.at[:, pl.ds(to, rows)], load_sem.at[i]
        )
        for i, (at, rows, to) in enumerate(
            ((0, 96, FSTEPS), (96 - FSTEPS, FSTEPS, 0), (0, FSTEPS, FSTEPS + 96))
        )
    ]
    for cp in loads:
        cp.start()

    barrier = pltpu.get_barrier_semaphore()

    def greet(tm, space):
        pl.semaphore_signal(barrier, inc=1, device_id=(tm, space), device_id_type=MESH)

    for j in range(1, 8):
        greet(n, (sp + j) % 8)

    @pl.when(hub != n)
    def _():
        greet(hub, sp)

    @pl.when(is_chain)
    def _():
        def spoke(i, _):
            @pl.when(first_slice + i != n)
            def _():
                greet(first_slice + i, sp)

            return 0

        lax.fori_loop(0, size, spoke, 0)

        @pl.when(role > 0)
        def _():
            for off in (-2, -1, 0, 1, 2):
                other = (tile + off) % 8
                before = place(role - 1, other)
                greet(before, space_of(other, before))

    spokes = size - jnp.where(in_own, 1, 0) + jnp.where(role < BLOCKS - 1, 5, 0)
    pl.semaphore_wait(barrier, 7 + jnp.where(hub != n, 1, 0) + jnp.where(is_chain, spokes, 0))

    for cp in loads:
        cp.wait()
    copies = []
    for j in range(1, 8):
        to = (sp + j) % 8
        cp = pltpu.make_async_remote_copy(
            src_ref=wrapped.at[:, pl.ds(TILE * tile_of(to, n), WIDE)],
            dst_ref=gathered.at[pl.ds(2 * sp, 2)],
            send_sem=slab_send.at[j],
            recv_sem=slab_recv.at[j],
            device_id=(n, to),
            device_id_type=MESH,
        )
        cp.start()
        copies.append(cp)
    own = pltpu.make_async_copy(
        wrapped.at[:, pl.ds(TILE * tile, WIDE)], gathered.at[pl.ds(2 * sp, 2)], slab_recv.at[0]
    )
    own.start()
    own.wait()
    for cp in copies:
        cp.wait_recv()

    flat = gathered.reshape(16 * WIDE, 128)
    for y in range(WIDE):
        u[y, 0:8] = flat[pl.ds(y, 8, stride=2 * WIDE), :]
        u[y, 8:16] = flat[pl.ds(WIDE + y, 8, stride=2 * WIDE), :]
    own_rows = slice(FSTEPS, FSTEPS + TILE)
    step(u, v, FSTEPS, FSTEPS + TILE, 0.15, 0.1)
    deltas_own[...] = v[own_rows]
    a, b = u, v
    for i in range(FSTEPS):
        step(a, b, i + 1, WIDE - 1 - i, 0.03, 0.02)
        a, b = b, a
    fine[...] = a[own_rows]
    deltas_own[...] = a[own_rows] - deltas_own[...]

    def spread(src, dst_of, recv, to_block, ghost, sends, act):
        near, far = min(ghost, TILE), max(ghost - TILE, 0)
        parts = [(0, 0, TILE, GHOST)]
        if near:
            parts = [(1, TILE - near, near, GHOST - near), (7, 0, near, GHOST + TILE)] + parts
        if far:
            parts = [(2, TILE - far, far, GHOST - TILE - far), (6, 0, far, GHOST + 2 * TILE)] + parts
        for off, at, rows, to in parts:
            dest = (tile + off) % 8
            tm = place(to_block, dest)
            space = space_of(dest, tm)
            src_part, dst_part = src.at[pl.ds(at, rows)], dst_of.at[pl.ds(to, rows)]
            far_copy = pltpu.make_async_remote_copy(
                src_ref=src_part,
                dst_ref=dst_part,
                send_sem=spread_send.at[sends, off],
                recv_sem=recv,
                device_id=(tm, space),
                device_id_type=MESH,
            )
            if off:
                act(far_copy)
            else:
                mine = tm == n

                @pl.when(jnp.logical_not(mine))
                def _():
                    act(far_copy)

                if act is start:

                    @pl.when(mine)
                    def _():
                        pltpu.make_async_copy(src_part, dst_part, recv).start()

    def start(cp):
        cp.start()

    def finish(cp):
        cp.wait_send()

    def spread_deltas(act):
        for rem in range(GHOST):

            @pl.when(jnp.logical_and(left == rem, n > 0))
            def _():
                spread(deltas_own, deltas.at[rem], delta_recv.at[rem], block, rem, 0, act)

    def spread_first(act):
        @pl.when(n == 0)
        def _():
            spread(fine, c, state_recv, 0, SIZES[0] - 1, 1, act)

    spread_first(start)
    spread_deltas(start)
    spread_first(finish)
    spread_deltas(finish)

    flat_out = out_rows.reshape(GHOST * 16 * 16, 128)

    @pl.when(is_chain)
    def _():
        for b in range(BLOCKS):

            @pl.when(role == b)
            def _():
                whole = s.at[pl.ds(0, TILE + 2 * (SIZES[b] if b else SIZES[0] - 1))]
                pltpu.make_async_copy(whole, whole, state_recv).wait()

        def keep_for(rem):
            def keep(y, h, out):
                if GHOST <= y < GHOST + TILE:
                    flat_out[pl.ds(rem * 256 + 16 * h + y - GHOST, 8, stride=32), :] = out

            return keep

        for rem in reversed(range(GHOST)):
            src, dst = (s, c) if rem % 2 else (c, s)
            runs = rem < size
            if rem == SIZES[0] - 1:
                runs = jnp.logical_and(runs, role > 0)

                @pl.when(role == 0)
                def _(rem=rem):
                    for y in range(GHOST, GHOST + TILE):
                        for h in range(2):
                            keep_for(rem)(y, h, c[y, 8 * h : 8 * h + 8])

            @pl.when(runs)
            def _(rem=rem, src=src, dst=dst):
                whole = deltas.at[rem, pl.ds(0, TILE + 2 * rem)]
                pltpu.make_async_copy(whole, whole, delta_recv.at[rem]).wait()
                step(
                    src, dst, GHOST - rem, GHOST + TILE + rem, 0.15, 0.1,
                    lambda y, h: deltas[rem, y, h], keep_for(rem),
                )

        mid = s.at[pl.ds(GHOST, TILE)]

        def pass_on(act):
            for b in range(BLOCKS - 1):

                @pl.when(role == b)
                def _():
                    spread(mid, s, state_recv, b + 1, SIZES[b + 1], 1, act)

        pass_on(start)

        def send(i, _):
            away = 4 + (i + 1) // 2 * (1 - 2 * (i % 2))
            for at in range(2):
                tm = (first_slice // 8 + at) * 8 + (n + away) % 8
                rem = first_slice + size - 1 - tm

                @pl.when(jnp.logical_and(rem >= 0, rem < size))
                def _():
                    for off in range(8):
                        to = (sp + off) % 8
                        src = out_rows.at[pl.ds(16 * rem + 2 * to, 2), pl.ds(0, TILE)]
                        dst = o_ref.at[0, :, pl.ds(TILE * tile, TILE)]
                        remote = pltpu.make_async_remote_copy(
                            src_ref=src,
                            dst_ref=dst,
                            send_sem=ends_send,
                            recv_sem=ends_recv,
                            device_id=(tm, to),
                            device_id_type=MESH,
                        )
                        if off:
                            remote.start()
                        else:

                            @pl.when(tm == n)
                            def _():
                                pltpu.make_async_copy(src, dst, ends_recv).start()

                            @pl.when(tm != n)
                            def _():
                                remote.start()

            return 0

        lax.fori_loop(0, 8, send, 0)
        pass_on(finish)
        for b in range(BLOCKS):

            for own in range(2):

                @pl.when(jnp.logical_and(role == b, in_own == bool(own)))
                def _():
                    count = 8 * SIZES[b] - own
                    sent = out_rows.at[pl.ds(0, 2 * count), pl.ds(0, TILE)]
                    pltpu.make_async_copy(sent, sent, ends_send).wait()

    for cp in copies:
        cp.wait_send()
    pltpu.make_async_copy(o_ref, o_ref, ends_recv).wait()


def per_device(starts):
    field = jnp.float32
    dma = pltpu.SemaphoreType.DMA
    return pl.pallas_call(
        kernel,
        out_shape=jax.ShapeDtypeStruct(starts.shape, starts.dtype),
        in_specs=[pl.BlockSpec(memory_space=pl.ANY)],
        out_specs=pl.BlockSpec(memory_space=pl.ANY),
        scratch_shapes=[
            pltpu.VMEM((2, 96 + 2 * FSTEPS, 128), field),
            pltpu.VMEM((16, WIDE, 128), field),
            pltpu.VMEM((WIDE, 16, 128), field),
            pltpu.VMEM((WIDE, 16, 128), field),
            pltpu.VMEM((TILE, 16, 128), field),
            pltpu.VMEM((TILE, 16, 128), field),
            pltpu.VMEM((GHOST, SPAN, 16, 128), field),
            pltpu.VMEM((SPAN, 16, 128), field),
            pltpu.VMEM((SPAN, 16, 128), field),
            pltpu.VMEM((GHOST * 16, 16, 128), field),
            dma((8,)),
            dma((8,)),
            dma((2, 8)),
            dma((GHOST,)),
            dma,
            dma,
            dma,
            dma((3,)),
        ],
        compiler_params=pltpu.CompilerParams(
            collective_id=0, has_side_effects=True, vmem_limit_bytes=40 << 20
        ),
    )(starts)


def solution(mesh):
    placed = P("tm", "space", None, None)
    return jax.shard_map(
        per_device, mesh=mesh, in_specs=(placed,), out_specs=placed, check_vma=False
    )
```

time: 83.2 us -> 73.7 us (0.89)
  the two profiles are of different devices: /device:TPU:511 before, /device:TPU:263 now
where the time goes in v4:
time: 73.7 us; the launch traced here: 73.6 us
  Pallas kernels  72 us (98%)
  local copies, waits for them, and re-layouts  1.54 us (2%)
    pallas_call x1, Pallas kernels, per_device(): pl.pallas_call(kernel, out_shape=jax.ShapeDtypeStruct(starts.shape, start...  72 us
    unnamed x3, local copies, waits for them, and re-layouts  1.54 us

profile of v4, /device:TPU:263, one launch (start us, length us, event | category | flops | bytes accessed | tf_op | source)
XLA Modules:
  0.0 73.6 jit_solution(12775881065002225955)
XLA Ops:
  0.0 0.0 copy-start
  0.0 0.9 %copy-done = f32[1,2,96,128]{3,2,1,0:T(8,128)S(1)} copy-done((f32[1,2,96,128]{3,2,1,0:T(8,128)S(1)}, f32[1,2,96,128]{3,2,1,0:T(8,128)}, u32[]{:S(2)}) %copy-start) | copy-done | bytes 98328
  0.9 72.0 %shard_map.17 = f32[1,2,96,128]{3,2,1,0:T(8,128)S(1)} custom-call(f32[1,2,96,128]{3,2,1,0:T(8,128)S(1)} %copy-done), custom_call_target="tpu_custom_call" | custom-call | tf_op jit(solution)/shard_map/pallas_call | solution.py:325
  72.9 0.6 copy.3
Async XLA Ops:
  0.0 0.9 %copy-start = (f32[1,2,96,128]{3,2,1,0:T(8,128)S(1)}, f32[1,2,96,128]{3,2,1,0:T(8,128)}, u32[]{:S(2)}) copy-start(f32[1,2,96,128]{3,2,1,0:T(8,128)} %x_ref.1) | copy-start | bytes 294916

commit v5 on v4

--- a/solution.py
+++ b/solution.py
@@ -13,6 +13,8 @@
 BLOCKS = len(STARTS) - 1
 SIZES = tuple(STARTS[b + 1] - STARTS[b] for b in range(BLOCKS))
 GHOST = max(SIZES)
+SPREAD = max((STARTS[b + 1] - 1) // 8 - STARTS[b] // 8 + 1 for b in range(BLOCKS))
+CUTS = sorted({0, 4, SIZES[0] - 1, *SIZES})
 PLACES = ((0, 0), (8, 8), (24, 24), (32, 40), (56, 48))
 TILE = 12
 WIDE = TILE + 2 * FSTEPS
@@ -146,7 +148,7 @@
     for cp in copies:
         cp.wait_recv()
 
-    flat = gathered.reshape(16 * WIDE, 128)
+    flat = gathered.reshape(18 * WIDE, 128)
     for y in range(WIDE):
         u[y, 0:8] = flat[pl.ds(y, 8, stride=2 * WIDE), :]
         u[y, 8:16] = flat[pl.ds(WIDE + y, 8, stride=2 * WIDE), :]
@@ -218,10 +220,46 @@
     spread_first(finish)
     spread_deltas(finish)
 
-    flat_out = out_rows.reshape(GHOST * 16 * 16, 128)
+    flat_out = out_rows.reshape((GHOST * 16 + 2) * 16, 128)
 
     @pl.when(is_chain)
     def _():
+        def send(tm):
+            rem = first_slice + size - 1 - tm
+
+            @pl.when(jnp.logical_and(rem >= 0, rem < size))
+            def _():
+                for off in range(8):
+                    to = (sp + off) % 8
+                    src = out_rows.at[pl.ds(16 * rem + 2 * to, 2), pl.ds(0, TILE)]
+                    dst = o_ref.at[0, :, pl.ds(TILE * tile, TILE)]
+                    remote = pltpu.make_async_remote_copy(
+                        src_ref=src,
+                        dst_ref=dst,
+                        send_sem=ends_send,
+                        recv_sem=ends_recv,
+                        device_id=(tm, to),
+                        device_id_type=MESH,
+                    )
+                    if off:
+                        remote.start()
+                    else:
+
+                        @pl.when(tm == n)
+                        def _():
+                            pltpu.make_async_copy(src, dst, ends_recv).start()
+
+                        @pl.when(tm != n)
+                        def _():
+                            remote.start()
+
+        for rem in reversed(range(GHOST)):
+
+            @pl.when(rem < size - jnp.where(role == 0, 1, 0))
+            def _(rem=rem):
+                whole = deltas.at[rem, pl.ds(0, TILE + 2 * rem)]
+                pltpu.make_async_copy(whole, whole, delta_recv.at[rem]).wait()
+
         for b in range(BLOCKS):
 
             @pl.when(role == b)
@@ -236,26 +274,30 @@
 
             return keep
 
-        for rem in reversed(range(GHOST)):
-            src, dst = (s, c) if rem % 2 else (c, s)
-            runs = rem < size
-            if rem == SIZES[0] - 1:
-                runs = jnp.logical_and(runs, role > 0)
-
-                @pl.when(role == 0)
-                def _(rem=rem):
-                    for y in range(GHOST, GHOST + TILE):
-                        for h in range(2):
-                            keep_for(rem)(y, h, c[y, 8 * h : 8 * h + 8])
-
-            @pl.when(runs)
-            def _(rem=rem, src=src, dst=dst):
-                whole = deltas.at[rem, pl.ds(0, TILE + 2 * rem)]
-                pltpu.make_async_copy(whole, whole, delta_recv.at[rem]).wait()
-                step(
-                    src, dst, GHOST - rem, GHOST + TILE + rem, 0.15, 0.1,
-                    lambda y, h: deltas[rem, y, h], keep_for(rem),
-                )
+        @pl.when(role == 0)
+        def _():
+            for y in range(GHOST, GHOST + TILE):
+                for h in range(2):
+                    keep_for(SIZES[0] - 1)(y, h, c[y, 8 * h : 8 * h + 8])
+
+        for low, high in reversed(list(zip(CUTS, CUTS[1:]))):
+
+            @pl.when(high <= size - jnp.where(role == 0, 1, 0))
+            def _(low=low, high=high):
+                for rem in reversed(range(low, high)):
+                    src, dst = (s, c) if rem % 2 else (c, s)
+                    step(
+                        src, dst, GHOST - rem, GHOST + TILE + rem, 0.15, 0.1,
+                        lambda y, h, rem=rem: deltas[rem, y, h], keep_for(rem),
+                    )
+
+                @pl.when(role == BLOCKS - 1)
+                def _():
+                    def stretch(i, _):
+                        send(first_slice + size - high + i)
+                        return 0
+
+                    lax.fori_loop(0, high - low, stretch, 0)
 
         mid = s.at[pl.ds(GHOST, TILE)]
 
@@ -268,41 +310,16 @@
 
         pass_on(start)
 
-        def send(i, _):
-            away = 4 + (i + 1) // 2 * (1 - 2 * (i % 2))
-            for at in range(2):
-                tm = (first_slice // 8 + at) * 8 + (n + away) % 8
-                rem = first_slice + size - 1 - tm
-
-                @pl.when(jnp.logical_and(rem >= 0, rem < size))
-                def _():
-                    for off in range(8):
-                        to = (sp + off) % 8
-                        src = out_rows.at[pl.ds(16 * rem + 2 * to, 2), pl.ds(0, TILE)]
-                        dst = o_ref.at[0, :, pl.ds(TILE * tile, TILE)]
-                        remote = pltpu.make_async_remote_copy(
-                            src_ref=src,
-                            dst_ref=dst,
-                            send_sem=ends_send,
-                            recv_sem=ends_recv,
-                            device_id=(tm, to),
-                            device_id_type=MESH,
-                        )
-                        if off:
-                            remote.start()
-                        else:
-
-                            @pl.when(tm == n)
-                            def _():
-                                pltpu.make_async_copy(src, dst, ends_recv).start()
-
-                            @pl.when(tm != n)
-                            def _():
-                                remote.start()
-
-            return 0
-
-        lax.fori_loop(0, 8, send, 0)
+        @pl.when(role < BLOCKS - 1)
+        def _():
+            def around(i, _):
+                away = 4 + (i + 1) // 2 * (1 - 2 * (i % 2))
+                for at in range(SPREAD):
+                    send((first_slice // 8 + at) * 8 + (n + away) % 8)
+                return 0
+
+            lax.fori_loop(0, 8, around, 0)
+
         pass_on(finish)
         for b in range(BLOCKS):
 
@@ -329,7 +346,7 @@
         out_specs=pl.BlockSpec(memory_space=pl.ANY),
         scratch_shapes=[
             pltpu.VMEM((2, 96 + 2 * FSTEPS, 128), field),
-            pltpu.VMEM((16, WIDE, 128), field),
+            pltpu.VMEM((18, WIDE, 128), field),
             pltpu.VMEM((WIDE, 16, 128), field),
             pltpu.VMEM((WIDE, 16, 128), field),
             pltpu.VMEM((TILE, 16, 128), field),
@@ -337,7 +354,7 @@
             pltpu.VMEM((GHOST, SPAN, 16, 128), field),
             pltpu.VMEM((SPAN, 16, 128), field),
             pltpu.VMEM((SPAN, 16, 128), field),
-            pltpu.VMEM((GHOST * 16, 16, 128), field),
+            pltpu.VMEM((GHOST * 16 + 2, 16, 128), field),
             dma((8,)),
             dma((8,)),
             dma((2, 8)),

time: 73.7 us -> 69.7 us (0.946)
  the two profiles are of different devices: /device:TPU:263 before, /device:TPU:311 now
where the time goes in v5:
time: 69.7 us; the launch traced here: 69.6 us
  Pallas kernels  68.1 us (98%)
  local copies, waits for them, and re-layouts  1.54 us (2%)
    pallas_call x1, Pallas kernels, per_device(): pl.pallas_call(kernel, out_shape=jax.ShapeDtypeStruct(starts.shape, start...  68.1 us
    unnamed x3, local copies, waits for them, and re-layouts  1.54 us

profile of v5, /device:TPU:311, one launch (start us, length us, event | category | flops | bytes accessed | tf_op | source)
XLA Modules:
  0.0 69.6 jit_solution(5979294373722149696)
XLA Ops:
  0.0 0.0 copy-start
  0.0 0.9 %copy-done = f32[1,2,96,128]{3,2,1,0:T(8,128)S(1)} copy-done((f32[1,2,96,128]{3,2,1,0:T(8,128)S(1)}, f32[1,2,96,128]{3,2,1,0:T(8,128)}, u32[]{:S(2)}) %copy-start) | copy-done | bytes 98328
  0.9 68.1 %shard_map.17 = f32[1,2,96,128]{3,2,1,0:T(8,128)S(1)} custom-call(f32[1,2,96,128]{3,2,1,0:T(8,128)S(1)} %copy-done), custom_call_target="tpu_custom_call" | custom-call | tf_op jit(solution)/shard_map/pallas_call | solution.py:342
  69.0 0.6 copy.3
Async XLA Ops:
  0.0 0.9 %copy-start = (f32[1,2,96,128]{3,2,1,0:T(8,128)S(1)}, f32[1,2,96,128]{3,2,1,0:T(8,128)}, u32[]{:S(2)}) copy-start(f32[1,2,96,128]{3,2,1,0:T(8,128)} %x_ref.1) | copy-start | bytes 294916

commit v6 on v5

--- a/solution.py
+++ b/solution.py
@@ -15,7 +15,8 @@
 GHOST = max(SIZES)
 SPREAD = max((STARTS[b + 1] - 1) // 8 - STARTS[b] // 8 + 1 for b in range(BLOCKS))
 CUTS = sorted({0, 4, SIZES[0] - 1, *SIZES})
-PLACES = ((0, 0), (8, 8), (24, 24), (32, 40), (56, 48))
+FIRST_ROWS = (0, 1, 2, 3, 7, 6, 5, 4)
+PLACES = ((0, 0), (8, 8), (24, 16), (32, 40), (56, 48))
 TILE = 12
 WIDE = TILE + 2 * FSTEPS
 SPAN = TILE + 2 * GHOST
@@ -56,7 +57,8 @@
 
 def place(block, tile):
     low = table([at[0] for at in PLACES], block)
-    return tile + jnp.where(tile < 4, low, table([at[1] for at in PLACES], block))
+    row = jnp.where(block == 0, table(FIRST_ROWS, tile), tile)
+    return row + jnp.where(tile < 4, low, table([at[1] for at in PLACES], block))
 
 
 def table(values, at):

time: 69.7 us -> 68.2 us (0.978)
  Pallas kernels: 68.1 us -> 66.5 us
    pallas_call x1, Pallas kernels: 68.1 us -> 66.5 us  [per_device(): pl.pallas_call(kernel, out_shape=jax.ShapeDtypeStruct(starts.shape, start...]
where the time goes in v6:
time: 68.2 us; the launch traced here: 68.1 us
  Pallas kernels  66.5 us (98%)
  local copies, waits for them, and re-layouts  1.54 us (2%)
    pallas_call x1, Pallas kernels, per_device(): pl.pallas_call(kernel, out_shape=jax.ShapeDtypeStruct(starts.shape, start...  66.5 us
    unnamed x3, local copies, waits for them, and re-layouts  1.54 us

profile of v6, /device:TPU:311, one launch (start us, length us, event | category | flops | bytes accessed | tf_op | source)
XLA Modules:
  0.0 68.1 jit_solution(11963613711461573662)
XLA Ops:
  0.0 0.0 copy-start
  0.0 0.9 %copy-done = f32[1,2,96,128]{3,2,1,0:T(8,128)S(1)} copy-done((f32[1,2,96,128]{3,2,1,0:T(8,128)S(1)}, f32[1,2,96,128]{3,2,1,0:T(8,128)}, u32[]{:S(2)}) %copy-start) | copy-done | bytes 98328
  0.9 66.5 %shard_map.17 = f32[1,2,96,128]{3,2,1,0:T(8,128)S(1)} custom-call(f32[1,2,96,128]{3,2,1,0:T(8,128)S(1)} %copy-done), custom_call_target="tpu_custom_call" | custom-call | tf_op jit(solution)/shard_map/pallas_call | solution.py:344
  67.4 0.6 copy.3
Async XLA Ops:
  0.0 0.9 %copy-start = (f32[1,2,96,128]{3,2,1,0:T(8,128)S(1)}, f32[1,2,96,128]{3,2,1,0:T(8,128)}, u32[]{:S(2)}) copy-start(f32[1,2,96,128]{3,2,1,0:T(8,128)} %x_ref.1) | copy-start | bytes 294916

commit v7 on v6

--- a/solution.py
+++ b/solution.py
@@ -14,8 +14,8 @@
 SIZES = tuple(STARTS[b + 1] - STARTS[b] for b in range(BLOCKS))
 GHOST = max(SIZES)
 SPREAD = max((STARTS[b + 1] - 1) // 8 - STARTS[b] // 8 + 1 for b in range(BLOCKS))
-CUTS = sorted({0, 4, SIZES[0] - 1, *SIZES})
-FIRST_ROWS = (0, 1, 2, 3, 7, 6, 5, 4)
+CUTS = sorted({0, 2, 4, SIZES[0] - 1, *SIZES})
+FIRST_ROWS = (1, 1, 2, 2, 6, 6, 5, 5)
 PLACES = ((0, 0), (8, 8), (24, 16), (32, 40), (56, 48))
 TILE = 12
 WIDE = TILE + 2 * FSTEPS
@@ -130,8 +130,8 @@
     for cp in loads:
         cp.wait()
     copies = []
-    for j in range(1, 8):
-        to = (sp + j) % 8
+    for j, (dz, flip) in enumerate(((2, 0), (2, 1), (3, 0), (3, 1), (1, 0), (1, 1), (0, 1)), 1):
+        to = (sp // 2 + dz) % 4 * 2 + (sp + flip) % 2
         cp = pltpu.make_async_remote_copy(
             src_ref=wrapped.at[:, pl.ds(TILE * tile_of(to, n), WIDE)],
             dst_ref=gathered.at[pl.ds(2 * sp, 2)],

time: 68.2 us -> 68 us (level)
  no operation moved by 1% of the time
where the time goes in v7:
time: 68 us; the launch traced here: 67.9 us
  Pallas kernels  66.3 us (98%)
  local copies, waits for them, and re-layouts  1.54 us (2%)
    pallas_call x1, Pallas kernels, per_device(): pl.pallas_call(kernel, out_shape=jax.ShapeDtypeStruct(starts.shape, start...  66.3 us
    unnamed x3, local copies, waits for them, and re-layouts  1.54 us

profile of v7, /device:TPU:311, one launch (start us, length us, event | category | flops | bytes accessed | tf_op | source)
XLA Modules:
  0.0 67.9 jit_solution(12116741654717506540)
XLA Ops:
  0.0 0.0 copy-start
  0.0 0.9 %copy-done = f32[1,2,96,128]{3,2,1,0:T(8,128)S(1)} copy-done((f32[1,2,96,128]{3,2,1,0:T(8,128)S(1)}, f32[1,2,96,128]{3,2,1,0:T(8,128)}, u32[]{:S(2)}) %copy-start) | copy-done | bytes 98328
  0.9 66.3 %shard_map.17 = f32[1,2,96,128]{3,2,1,0:T(8,128)S(1)} custom-call(f32[1,2,96,128]{3,2,1,0:T(8,128)S(1)} %copy-done), custom_call_target="tpu_custom_call" | custom-call | tf_op jit(solution)/shard_map/pallas_call | solution.py:344
  67.2 0.6 copy.3
Async XLA Ops:
  0.0 0.9 %copy-start = (f32[1,2,96,128]{3,2,1,0:T(8,128)S(1)}, f32[1,2,96,128]{3,2,1,0:T(8,128)}, u32[]{:S(2)}) copy-start(f32[1,2,96,128]{3,2,1,0:T(8,128)} %x_ref.1) | copy-start | bytes 294916

commit v8 on v7

--- a/solution.py
+++ b/solution.py
@@ -17,13 +17,14 @@
 CUTS = sorted({0, 2, 4, SIZES[0] - 1, *SIZES})
 FIRST_ROWS = (1, 1, 2, 2, 6, 6, 5, 5)
 PLACES = ((0, 0), (8, 8), (24, 16), (32, 40), (56, 48))
+SCALE = (2.0 / 3.0) ** 0.5
 TILE = 12
 WIDE = TILE + 2 * FSTEPS
 SPAN = TILE + 2 * GHOST
 
 
 def step(src, dst, first, last, rate, react, more=None, keep=None):
-    stay = 1.0 - 6.0 * rate + react
+    stay = (1.0 - 6.0 * rate + react) / rate
     halves = (slice(0, 8), slice(8, 16))
     below = [src[first - 1, h] for h in halves]
     here = [src[first, h] for h in halves]
@@ -36,7 +37,7 @@
                 + (below[h] + above[h])
                 + (pltpu.roll(v, 1, 1) + pltpu.roll(v, 127, 1))
             )
-            out = v * (stay - react * (v * v)) + rate * beside
+            out = rate * (v * (stay - v * v) + beside)
             if more is not None:
                 out = out + more(y, halves[h])
             dst[y, halves[h]] = out
@@ -152,8 +153,8 @@
 
     flat = gathered.reshape(18 * WIDE, 128)
     for y in range(WIDE):
-        u[y, 0:8] = flat[pl.ds(y, 8, stride=2 * WIDE), :]
-        u[y, 8:16] = flat[pl.ds(WIDE + y, 8, stride=2 * WIDE), :]
+        u[y, 0:8] = SCALE * flat[pl.ds(y, 8, stride=2 * WIDE), :]
+        u[y, 8:16] = SCALE * flat[pl.ds(WIDE + y, 8, stride=2 * WIDE), :]
     own_rows = slice(FSTEPS, FSTEPS + TILE)
     step(u, v, FSTEPS, FSTEPS + TILE, 0.15, 0.1)
     deltas_own[...] = v[own_rows]
@@ -272,7 +273,7 @@
         def keep_for(rem):
             def keep(y, h, out):
                 if GHOST <= y < GHOST + TILE:
-                    flat_out[pl.ds(rem * 256 + 16 * h + y - GHOST, 8, stride=32), :] = out
+                    flat_out[pl.ds(rem * 256 + 16 * h + y - GHOST, 8, stride=32), :] = out * (1.0 / SCALE)
 
             return keep
 

time: 68 us -> 68.1 us (level)
  no operation moved by 1% of the time
where the time goes in v8:
time: 68.1 us; the launch traced here: 68 us
  Pallas kernels  66.4 us (98%)
  local copies, waits for them, and re-layouts  1.54 us (2%)
    pallas_call x1, Pallas kernels, per_device(): pl.pallas_call(kernel, out_shape=jax.ShapeDtypeStruct(starts.shape, start...  66.4 us
    unnamed x3, local copies, waits for them, and re-layouts  1.54 us

profile of v8, /device:TPU:311, one launch (start us, length us, event | category | flops | bytes accessed | tf_op | source)
XLA Modules:
  0.0 68.0 jit_solution(17944146296316185988)
XLA Ops:
  0.0 0.0 copy-start
  0.0 0.9 %copy-done = f32[1,2,96,128]{3,2,1,0:T(8,128)S(1)} copy-done((f32[1,2,96,128]{3,2,1,0:T(8,128)S(1)}, f32[1,2,96,128]{3,2,1,0:T(8,128)}, u32[]{:S(2)}) %copy-start) | copy-done | bytes 98328
  0.9 66.4 %shard_map.17 = f32[1,2,96,128]{3,2,1,0:T(8,128)S(1)} custom-call(f32[1,2,96,128]{3,2,1,0:T(8,128)S(1)} %copy-done), custom_call_target="tpu_custom_call" | custom-call | tf_op jit(solution)/shard_map/pallas_call | solution.py:345
  67.3 0.6 copy.3
Async XLA Ops:
  0.0 0.9 %copy-start = (f32[1,2,96,128]{3,2,1,0:T(8,128)S(1)}, f32[1,2,96,128]{3,2,1,0:T(8,128)}, u32[]{:S(2)}) copy-start(f32[1,2,96,128]{3,2,1,0:T(8,128)} %x_ref.1) | copy-start | bytes 294916
